TPU v7x, 32 devices: a whole 2x2x4 slice. The times are simulated.
32 devices in a mesh: groups: 2 (over x), row: 16 (over z, y, core).
Axes of the slice: x: 2, y: 2, z: 4, core: 2. Of those that a mesh axis runs over, the one named last changes fastest.
Arguments:
- basis: float32 [8192, 128], P(('groups', 'row')), parts along dimension 0, may hold values from -6 to 6
- springs: float32 [8192], P(('groups', 'row')), parts along dimension 0, may hold values from 0.25 to 8
- tangent_blocks: float32 [4096, 4096], P(('groups', 'row')), parts along dimension 0, may hold values from -0.375 to 0.375
- tile_rows: int32 [4096], P(('groups', 'row')), parts along dimension 0, may hold values from 0 to 3
- tile_owner: int32 [4096, 1], P(('groups', 'row')), parts along dimension 0, may hold values from 0 to 15, as said below
- tile_offset: int32 [4096], P(('groups', 'row')), parts along dimension 0, may hold values from 0 to 3
- tile_count: int32 [32], P(('groups', 'row')), parts along dimension 0, may hold values from 32 to 128, as said below
Outputs:
- stiff_image: float32 [8192, 128], P(('groups', 'row')), parts along dimension 0
- reduced: float32 [256, 128], P('groups'), parts along dimension 0
There are 2 independent parts, one for each index of `groups`. A program takes and returns all parts, laid end to end along the dimension named above; each array names one. Nothing has to cross between parts.
Inputs may be any that keep to these rules, and one draw needn't show every extreme that they name: The first tile_count[d] slots of device d are live; some device has exactly 128. `tile_owner`: the slab is closed into a shell: every slot of device d names owner (d + o) mod 16 with o one of 0, 1, -1, 4, -4, 5, -5, 8. Among the slots of one device no owner appears more than 32 times, and owner d itself appears exactly 32 times in every device.
All inputs are finite; a program needn't handle non-finite values.
Results may differ from a plain program's by a relative error of at most 0.0003.
Values sent between devices are 32-bit elements; how exact they have to be, the bound alone decides.
A program may use at most 128 MiB of HBM per device.

v0:
```python
import jax
import jax.numpy as jnp
from jax import lax
from jax.sharding import PartitionSpec as P

B = 64
MODES = 128
BR_DEV = 4
CAP = 128


def shards(basis, springs, tangent_blocks, tile_rows, tile_owner, tile_offset, tile_count):
    row_devices = lax.axis_size("row")
    dof_total = basis.shape[0] * row_devices
    own_blocks = basis.reshape(BR_DEV, B, MODES)
    square_blocks = tangent_blocks.reshape(CAP, B, B)
    owner_ids = tile_owner[:, 0]
    gathered = lax.all_gather(own_blocks, "row", axis=0, tiled=True)
    picked = gathered[owner_ids * BR_DEV + tile_offset]
    live_slot = (jnp.arange(CAP, dtype=jnp.int32) < tile_count[0]).astype(jnp.float32)
    row_ids = jnp.arange(BR_DEV, dtype=jnp.int32)
    products = jnp.einsum("sij,sjk->sik", square_blocks, picked, precision=lax.Precision.HIGHEST)
    row_select = (tile_rows[None, :] == row_ids[:, None]).astype(jnp.float32) * live_slot[None, :]
    summed = jnp.dot(row_select, products.reshape(CAP, B * MODES), precision=lax.Precision.HIGHEST)
    stiff_image = springs[:, None] * basis + summed.reshape(BR_DEV * B, MODES)
    partial_term = (
        jnp.einsum("rm,rn->mn", basis, stiff_image, precision=lax.Precision.HIGHEST) / dof_total
    )
    reduced = lax.psum(partial_term, "row")
    return (stiff_image, reduced)


def solution(mesh):
    in_specs = (
        P(("groups", "row"), None),
        P(("groups", "row")),
        P(("groups", "row"), None),
        P(("groups", "row")),
        P(("groups", "row"), None),
        P(("groups", "row")),
        P(("groups", "row")),
    )
    out_specs = (P(("groups", "row"), None), P("groups", None))
    return jax.shard_map(shards, mesh=mesh, in_specs=in_specs, out_specs=out_specs, check_vma=False)
```

profile of v0, /device:TPU:8, one launch (start us, length us, event | category | flops | bytes accessed | tf_op | source)
XLA Modules:
  0.0 163.7 jit_solution(6896301566178183216)
XLA Ops:
  7.2 0.0 all-gather.2.cloned.1.call-start
  7.2 0.7 all-gather.2.cloned.1.call-update
  7.9 0.0 all-reduce.2.cloned.1.call-start
  7.9 1.9 %copy.13 = f32[128,4096]{0,1:T(8,128)S(1)} copy(f32[128,4096]{1,0:T(8,128)} %param.9) | data formatting | bytes 4194304 | tf_op args[2]
  9.9 0.0 copy-start.4
  9.9 0.0 copy-start.5
  9.9 4.5 %copy.14 = f32[128,64,64]{2,1,0:T(8,128)} copy(f32[128,64,64]{0,2,1:T(8,128)S(1)} %bitcast.20) | data formatting | bytes 4194304 | tf_op jit(solution)/shard_map/reshape | solution.py:16
  15.1 0.0 copy-done.4
  15.1 0.0 copy-done.5
  15.1 36.7 %all-gather.2.cloned.1.call-done = f32[64,64,128]{2,1,0:T(8,128)} async-done(((f32[4,64,128]{2,1,0:T(8,128)}), f32[64,64,128]{2,1,0:T(8,128)}) %all-gather.2.cloned.1.call-update) | async-done | bytes 2097168 | tf_op jit(solution)/shard_map/all_gather | solution.py:18
  51.8 4.4 %gather_fusion = f32[128,64,128]{2,1,0:T(8,128)} fusion(f32[64,64,128]{2,1,0:T(8,128)} %all-gather.2.cloned.1.call-done, s32[1024]{0:T(1024)S(1)} %pad_clamp_fusion), kind=kCustom, calls=%fused_computation | custom fusion | bytes 8389120 | tf_op jit(solution)/shard_map/gather | solution.py:19
  56.1 0.0 copy-start.3
  56.1 6.5 %fusion.9 = f32[128,128,64]{1,2,0:T(8,128)S(1)} fusion(f32[128,64,128]{2,1,0:T(8,128)} %gather_fusion, f32[128,64,64]{2,1,0:T(8,128)} %copy.14), kind=kOutput, calls=%fused_computation.17 | convolution fusion | flops 805306368 | bytes 10485760 | tf_op jit(solution)/shard_map/sij,sjk->sik/dot_general | solution.py:22
  62.7 0.0 copy-start
  62.7 0.0 copy-start.2
  62.7 0.0 copy-done.3
  62.7 4.3 %fusion = f32[4,8192]{1,0:T(4,128)S(1)} fusion(f32[16,8,64,128]{3,2,1,0:T(8,128)S(1)} %bitcast.19, f32[128]{0:T(128)S(1)} %compare_convert_fusion, s32[128]{0:T(128)S(1)} %copy-done.3), kind=kOutput, calls=%fused_computation.1 | convolution fusion | flops 50332672 | bytes 4326400 | tf_op jit(solution)/shard_map/dot_general | solution.py:24
  67.1 0.1 reshape.28
  67.2 0.0 copy-done
  67.2 0.0 copy-done.2
  67.2 0.1 multiply_add_fusion
  67.3 0.0 copy-start.1
  67.3 1.0 fusion.3
  68.3 0.0 all-reduce.2.cloned.1.call-update
  68.3 86.9 %all-reduce.2.cloned.1.call-done = f32[128,128]{0,1:T(8,128)} async-done(((f32[128,128]{0,1:T(8,128)}), f32[128,128]{0,1:T(8,128)}) %all-reduce.2.cloned.1.call-update) | async-done | bytes 65552 | tf_op jit(solution)/shard_map/psum | solution.py:29
  155.3 1.6 copy.15
  156.8 0.0 copy-done.1
  (3 shorter events, 0.0 us)
Async XLA Ops:
  7.2 44.6 %all-gather.2.cloned.1.call-start = ((), (), s32[]{:S(2)}) async-start(), calls=%async_computation | async-start | bytes 2228224 | tf_op jit(solution)/shard_map/all_gather | solution.py:18
  7.9 147.4 %all-reduce.2.cloned.1.call-start = ((), (), s32[]{:S(2)}) async-start(), calls=%async_computation.1 | async-start | bytes 131072 | tf_op jit(solution)/shard_map/psum | solution.py:29
  9.9 5.2 %copy-start.4 = (s32[128]{0:T(128)S(1)}, s32[128]{0:T(128)}, u32[]{:S(2)}) copy-start(s32[128]{0:T(128)} %param.12) | copy-start | bytes 1540
  9.9 5.2 %copy-start.5 = (s32[128,1]{0,1:T(1,128)S(1)}, s32[128,1]{0,1:T(1,128)}, u32[]{:S(2)}) copy-start(s32[128,1]{0,1:T(1,128)} %param.11) | copy-start | bytes 1540
  56.1 6.6 %copy-start.3 = (s32[128]{0:T(128)S(1)}, s32[128]{0:T(128)}, u32[]{:S(2)}) copy-start(s32[128]{0:T(128)} %param.10) | copy-start | bytes 1540
  62.7 4.5 %copy-start = (f32[256,128]{1,0:T(8,128)S(1)}, f32[256,128]{1,0:T(8,128)}, u32[]{:S(2)}) copy-start(f32[256,128]{1,0:T(8,128)} %param.7) | copy-start | bytes 393220
  62.7 4.5 %copy-start.2 = (f32[256]{0:T(256)S(1)}, f32[256]{0:T(256)}, u32[]{:S(2)}) copy-start(f32[256]{0:T(256)} %param.8) | copy-start | bytes 3076
  67.3 89.5 %copy-start.1 = (f32[256,128]{1,0:T(8,128)}, f32[256,128]{1,0:T(8,128)S(1)}, u32[]{:S(2)}) copy-start(f32[256,128]{1,0:T(8,128)S(1)} %multiply_add_fusion) | copy-start | bytes 393220
Sparse Core Ops, SparseCore 0:
  10.2 41.5 all-gather.1
  68.5 86.7 all-reduce.1
where the time goes:
time: 164 us
  waiting for transfers between devices  124 us (76%)
  between operations  14.8 us (9%)
  local copies, waits for them, and re-layouts  12.5 us (8%)
  matrix products  11.9 us (7%)
    psum x1, waiting for transfers between devices, shards(): reduced = lax.psum(partial_term, 'row')  86.9 us
    all_gather x1, waiting for transfers between devices, shards(): gathered = lax.all_gather(own_blocks, 'row', axis=0, tiled=True)  36.7 us
    dot_general x1, matrix products, shards(): jnp.einsum('sij,sjk->sik', square_blocks, picked, precision=lax.Precision...  6.52 us
    reshape x1, local copies, waits for them, and re-layouts, shards(): square_blocks = tangent_blocks.reshape(CAP, B, B)  4.52 us
    gather x1, local copies, waits for them, and re-layouts, shards(): picked = gathered[owner_ids * BR_DEV + tile_offset]  4.35 us
    dot_general x1, matrix products, shards(): jnp.dot(row_select, products.reshape(CAP, B * MODES), precision=lax.Preci...  4.34 us
    unnamed x14, local copies, waits for them, and re-layouts  3.52 us
  transfers between devices with their start and end apart: 2, of which 2 were waited for; matrix products, arithmetic and copies ran while one was open for 4% of the time, Pallas kernels for 0%

commit v1 on v0

--- a/solution.py
+++ b/solution.py
@@ -2,6 +2,7 @@
 import jax.numpy as jnp
 from jax import lax
 from jax.sharding import PartitionSpec as P
+from jax.lax import axis_index, axis_size, ppermute
 
 B = 64
 MODES = 128
@@ -15,7 +16,31 @@
     own_blocks = basis.reshape(BR_DEV, B, MODES)
     square_blocks = tangent_blocks.reshape(CAP, B, B)
     owner_ids = tile_owner[:, 0]
-    gathered = lax.all_gather(own_blocks, "row", axis=0, tiled=True)
+
+    def serve_record_on(u):
+        answer, val2, all_rows = (axis_size("row"), axis_index("row"), u.shape[0])
+        kept_rows = [src_i * answer if q == 0 else src_i for q, src_i in enumerate(u.shape)]
+        block_out = res = u
+        arr_next = lax.dynamic_update_slice_in_dim(
+            jnp.zeros(kept_rows, u.dtype), u, val2 * all_rows, axis=0
+        )
+        for tick in range(1, answer // 2 + 1):
+            block_out = ppermute(
+                block_out, axis_name="row", perm=[(q, (q + 1) % answer) for q in range(answer)]
+            )
+            arr_next = lax.dynamic_update_slice_in_dim(
+                arr_next, block_out, (val2 - tick) % answer * all_rows, axis=0
+            )
+            if 2 * tick < answer:
+                res = ppermute(
+                    res, axis_name="row", perm=[(q, (q - 1) % answer) for q in range(answer)]
+                )
+                arr_next = lax.dynamic_update_slice_in_dim(
+                    arr_next, res, (val2 + tick) % answer * all_rows, axis=0
+                )
+        return arr_next
+
+    gathered = serve_record_on(own_blocks)
     picked = gathered[owner_ids * BR_DEV + tile_offset]
     live_slot = (jnp.arange(CAP, dtype=jnp.int32) < tile_count[0]).astype(jnp.float32)
     row_ids = jnp.arange(BR_DEV, dtype=jnp.int32)

time: 164 us -> 179 us (1.091)
  starting transfers between devices: 0.08 us -> 18.6 us
  waiting for transfers between devices: 124 us -> 120 us
    all_gather x1 -> x0, waiting for transfers between devices: 36.7 us -> none  [shards(): gathered = lax.all_gather(own_blocks, 'row', axis=0, tiled=True)]
    ppermute x0 -> x15, waiting for transfers between devices: none -> 21.5 us  [the longest x8 21.5 us: serve_record_on(): ppermute(block_out, axis_name='row', perm=[(q, (q + 1) % answer) for q in...]
    ppermute x0 -> x15, starting transfers between devices: none -> 18.6 us  [the longest x7 18.5 us: serve_record_on(): ppermute(res, axis_name='row', perm=[(q, (q - 1) % answer) for q in range...]
    psum x1, waiting for transfers between devices: 86.9 us -> 98.6 us  [shards(): reduced = lax.psum(partial_term, 'row')]
    unnamed x14 -> x10, local copies, waits for them, and re-layouts: 3.52 us -> 4.15 us
  transfers between devices with their start and end apart: 2 -> 16, of which waited for: 2 -> 8; matrix products, arithmetic and copies ran while one was open for 4% -> 4% of each run, Pallas kernels for 0% -> 0%
where the time goes in v1:
time: 179 us
  waiting for transfers between devices  120 us (67%)
  starting transfers between devices  18.6 us (10%)
  between operations  15.2 us (8%)
  local copies, waits for them, and re-layouts  12 us (7%)
  matrix products  11.9 us (7%)
    psum x1, waiting for transfers between devices, shards(): reduced = lax.psum(partial_term, 'row')  98.6 us
    ppermute x8, waiting for transfers between devices, serve_record_on(): ppermute(block_out, axis_name='row', perm=[(q, (q + 1) % answer) for q in...  21.5 us
    ppermute x7, starting transfers between devices, serve_record_on(): ppermute(res, axis_name='row', perm=[(q, (q - 1) % answer) for q in range...  18.5 us
    dot_general x1, matrix products, shards(): jnp.einsum('sij,sjk->sik', square_blocks, picked, precision=lax.Precision...  6.52 us
    reshape x1, local copies, waits for them, and re-layouts, shards(): square_blocks = tangent_blocks.reshape(CAP, B, B)  4.54 us
    dot_general x1, matrix products, shards(): jnp.dot(row_select, products.reshape(CAP, B * MODES), precision=lax.Preci...  4.34 us
    unnamed x10, local copies, waits for them, and re-layouts  4.15 us
  transfers between devices with their start and end apart: 16, of which 8 were waited for; matrix products, arithmetic and copies ran while one was open for 4% of the time, Pallas kernels for 0%

profile of v1, /device:TPU:8, one launch (start us, length us, event | category | flops | bytes accessed | tf_op | source)
XLA Modules:
  0.0 178.6 jit_solution(14514599059317237900)
XLA Ops:
  7.2 0.0 all-reduce.2.cloned.1.call-start
  7.2 0.1 collective-permute-start
  7.3 2.6 %collective-permute-start.1 = (f32[4,64,128]{2,1,0:T(8,128)}, f32[4,64,128]{2,1,0:T(8,128)S(1)}, u32[]{:S(2)}, u32[]{:S(2)}) collective-permute-start(f32[4,64,128]{2,1,0:T(8,128)} %bitcast.22), channel_id=1, source_target_pairs={{0,15},{1,0},{2,1},{3,2},{4,3},{5,4},{6,5},{7,6},{8,7},{9,8},{10,9... | collective-permute-start | bytes 393224 | tf_op jit(solution)/shard_map/ppermute | solution.py:35
  9.9 0.7 compare_select_fusion
  11.5 1.9 %copy.10 = f32[128,4096]{0,1:T(8,128)S(1)} copy(f32[128,4096]{1,0:T(8,128)} %param.9) | data formatting | bytes 4194304 | tf_op args[2]
  13.4 4.5 %copy.11 = f32[128,64,64]{2,1,0:T(8,128)} copy(f32[128,64,64]{0,2,1:T(8,128)S(1)} %bitcast.20) | data formatting | bytes 4194304 | tf_op jit(solution)/shard_map/reshape | solution.py:17
  18.0 0.2 broadcast_in_dim.4
  18.2 0.7 copy-done
  18.9 0.1 collective-permute-start.2
  19.0 2.6 %collective-permute-start.3 = (f32[4,64,128]{2,1,0:T(8,128)S(1)}, f32[4,64,128]{2,1,0:T(8,128)S(1)}, u32[]{:S(2)}, u32[]{:S(2)}) collective-permute-start(f32[4,64,128]{2,1,0:T(8,128)S(1)} %collective-permute-done.1), channel_id=1, source_target_pairs={{0,15},{1,0},{2,1},{3,2},{4,3},{5,4},{6,5},{7,6},{8,7},{9,8},{10,9... | collective-permute-start | bytes 393224 | tf_op jit(solution)/shard_map/ppermute | solution.py:35
  21.7 2.7 %collective-permute-done.2 = f32[4,64,128]{2,1,0:T(8,128)S(1)} collective-permute-done((f32[4,64,128]{2,1,0:T(8,128)S(1)}, f32[4,64,128]{2,1,0:T(8,128)S(1)}, u32[]{:S(2)}, u32[]{:S(2)}) %collective-permute-start.2) | collective-permute-done | bytes 131104 | tf_op jit(solution)/shard_map/ppermute | solution.py:28
  24.4 2.6 %collective-permute-start.5 = (f32[4,64,128]{2,1,0:T(8,128)S(1)}, f32[4,64,128]{2,1,0:T(8,128)S(1)}, u32[]{:S(2)}, u32[]{:S(2)}) collective-permute-start(f32[4,64,128]{2,1,0:T(8,128)S(1)} %collective-permute-done.3), channel_id=1, source_target_pairs={{0,15},{1,0},{2,1},{3,2},{4,3},{5,4},{6,5},{7,6},{8,7},{9,8},{10,9... | collective-permute-start | bytes 393224 | tf_op jit(solution)/shard_map/ppermute | solution.py:35
  27.1 2.7 %collective-permute-done.4 = f32[4,64,128]{2,1,0:T(8,128)S(1)} collective-permute-done((f32[4,64,128]{2,1,0:T(8,128)S(1)}, f32[4,64,128]{2,1,0:T(8,128)S(1)}, u32[]{:S(2)}, u32[]{:S(2)}) %collective-permute-start.4) | collective-permute-done | bytes 131104 | tf_op jit(solution)/shard_map/ppermute | solution.py:28
  29.8 2.6 %collective-permute-start.7 = (f32[4,64,128]{2,1,0:T(8,128)S(1)}, f32[4,64,128]{2,1,0:T(8,128)S(1)}, u32[]{:S(2)}, u32[]{:S(2)}) collective-permute-start(f32[4,64,128]{2,1,0:T(8,128)S(1)} %collective-permute-done.5), channel_id=1, source_target_pairs={{0,15},{1,0},{2,1},{3,2},{4,3},{5,4},{6,5},{7,6},{8,7},{9,8},{10,9... | collective-permute-start | bytes 393224 | tf_op jit(solution)/shard_map/ppermute | solution.py:35
  32.4 2.7 %collective-permute-done.6 = f32[4,64,128]{2,1,0:T(8,128)S(1)} collective-permute-done((f32[4,64,128]{2,1,0:T(8,128)S(1)}, f32[4,64,128]{2,1,0:T(8,128)S(1)}, u32[]{:S(2)}, u32[]{:S(2)}) %collective-permute-start.6) | collective-permute-done | bytes 131104 | tf_op jit(solution)/shard_map/ppermute | solution.py:28
  35.2 2.6 %collective-permute-start.9 = (f32[4,64,128]{2,1,0:T(8,128)S(1)}, f32[4,64,128]{2,1,0:T(8,128)S(1)}, u32[]{:S(2)}, u32[]{:S(2)}) collective-permute-start(f32[4,64,128]{2,1,0:T(8,128)S(1)} %collective-permute-done.7), channel_id=1, source_target_pairs={{0,15},{1,0},{2,1},{3,2},{4,3},{5,4},{6,5},{7,6},{8,7},{9,8},{10,9... | collective-permute-start | bytes 393224 | tf_op jit(solution)/shard_map/ppermute | solution.py:35
  37.8 2.7 %collective-permute-done.8 = f32[4,64,128]{2,1,0:T(8,128)S(1)} collective-permute-done((f32[4,64,128]{2,1,0:T(8,128)S(1)}, f32[4,64,128]{2,1,0:T(8,128)S(1)}, u32[]{:S(2)}, u32[]{:S(2)}) %collective-permute-start.8) | collective-permute-done | bytes 131104 | tf_op jit(solution)/shard_map/ppermute | solution.py:28
  40.6 2.6 %collective-permute-start.11 = (f32[4,64,128]{2,1,0:T(8,128)S(1)}, f32[4,64,128]{2,1,0:T(8,128)S(1)}, u32[]{:S(2)}, u32[]{:S(2)}) collective-permute-start(f32[4,64,128]{2,1,0:T(8,128)S(1)} %collective-permute-done.9), channel_id=1, source_target_pairs={{0,15},{1,0},{2,1},{3,2},{4,3},{5,4},{6,5},{7,6},{8,7},{9,8},{10,9... | collective-permute-start | bytes 393224 | tf_op jit(solution)/shard_map/ppermute | solution.py:35
  43.2 2.7 %collective-permute-done.10 = f32[4,64,128]{2,1,0:T(8,128)S(1)} collective-permute-done((f32[4,64,128]{2,1,0:T(8,128)S(1)}, f32[4,64,128]{2,1,0:T(8,128)S(1)}, u32[]{:S(2)}, u32[]{:S(2)}) %collective-permute-start.10) | collective-permute-done | bytes 131104 | tf_op jit(solution)/shard_map/ppermute | solution.py:28
  46.0 2.6 %collective-permute-start.13 = (f32[4,64,128]{2,1,0:T(8,128)S(1)}, f32[4,64,128]{2,1,0:T(8,128)S(1)}, u32[]{:S(2)}, u32[]{:S(2)}) collective-permute-start(f32[4,64,128]{2,1,0:T(8,128)S(1)} %collective-permute-done.11), channel_id=1, source_target_pairs={{0,15},{1,0},{2,1},{3,2},{4,3},{5,4},{6,5},{7,6},{8,7},{9,8},{10,9... | collective-permute-start | bytes 393224 | tf_op jit(solution)/shard_map/ppermute | solution.py:35
  48.6 2.7 %collective-permute-done.12 = f32[4,64,128]{2,1,0:T(8,128)S(1)} collective-permute-done((f32[4,64,128]{2,1,0:T(8,128)S(1)}, f32[4,64,128]{2,1,0:T(8,128)S(1)}, u32[]{:S(2)}, u32[]{:S(2)}) %collective-permute-start.12) | collective-permute-done | bytes 131104 | tf_op jit(solution)/shard_map/ppermute | solution.py:28
  51.4 5.2 %collective-permute-done.14 = f32[4,64,128]{2,1,0:T(8,128)S(1)} collective-permute-done((f32[4,64,128]{2,1,0:T(8,128)S(1)}, f32[4,64,128]{2,1,0:T(8,128)S(1)}, u32[]{:S(2)}, u32[]{:S(2)}) %collective-permute-start.14) | collective-permute-done | bytes 131104 | tf_op jit(solution)/shard_map/ppermute | solution.py:28
  56.7 2.8 %gather_fusion = f32[128,64,128]{2,1,0:T(8,128)} fusion(f32[64,64,128]{2,1,0:T(8,128)S(1)} %constant_dynamic-update-slice_fusion, s32[1024]{0:T(1024)S(1)} %pad_clamp_fusion), kind=kCustom, calls=%fused_computation | custom fusion | bytes 8389120 | tf_op jit(solution)/shard_map/gather | solution.py:44
  59.4 6.5 %fusion.9 = f32[128,128,64]{1,2,0:T(8,128)S(1)} fusion(f32[128,64,128]{2,1,0:T(8,128)} %gather_fusion, f32[128,64,64]{2,1,0:T(8,128)} %copy.11), kind=kOutput, calls=%fused_computation.33 | convolution fusion | flops 805306368 | bytes 10485760 | tf_op jit(solution)/shard_map/sij,sjk->sik/dot_general | solution.py:47
  66.0 4.3 %fusion = f32[4,8192]{1,0:T(4,128)S(1)} fusion(f32[16,8,64,128]{3,2,1,0:T(8,128)S(1)} %bitcast.19, f32[128]{0:T(128)S(1)} %compare_convert_fusion, s32[128]{0:T(128)S(1)} %copy-done.3), kind=kOutput, calls=%fused_computation.1 | convolution fusion | flops 50332672 | bytes 4326400 | tf_op jit(solution)/shard_map/dot_general | solution.py:49
  70.3 0.1 reshape.28
  70.4 0.1 multiply_add_fusion
  70.5 0.0 copy-start.1
  70.6 1.0 fusion.3
  71.6 0.0 all-reduce.2.cloned.1.call-update
  71.6 98.6 %all-reduce.2.cloned.1.call-done = f32[128,128]{0,1:T(8,128)} async-done(((f32[128,128]{0,1:T(8,128)}), f32[128,128]{0,1:T(8,128)}) %all-reduce.2.cloned.1.call-update) | async-done | bytes 65552 | tf_op jit(solution)/shard_map/psum | solution.py:54
  170.2 1.6 copy.12
  (38 shorter events, 0.3 us)
Async XLA Ops:
  7.2 163.0 %all-reduce.2.cloned.1.call-start = ((), (), s32[]{:S(2)}) async-start(), calls=%async_computation | async-start | bytes 131072 | tf_op jit(solution)/shard_map/psum | solution.py:54
  7.2 11.7 %collective-permute-start = (f32[4,64,128]{2,1,0:T(8,128)}, f32[4,64,128]{2,1,0:T(8,128)S(1)}, u32[]{:S(2)}, u32[]{:S(2)}) collective-permute-start(f32[4,64,128]{2,1,0:T(8,128)} %bitcast.21), channel_id=1, source_target_pairs={{0,1},{1,2},{2,3},{3,4},{4,5},{5,6},{6,7},{7,8},{8,9},{9,10},{10,1... | collective-permute-start | bytes 393224 | tf_op jit(solution)/shard_map/ppermute | solution.py:28
  7.3 11.7 %collective-permute-start.1 = (f32[4,64,128]{2,1,0:T(8,128)}, f32[4,64,128]{2,1,0:T(8,128)S(1)}, u32[]{:S(2)}, u32[]{:S(2)}) collective-permute-start(f32[4,64,128]{2,1,0:T(8,128)} %bitcast.22), channel_id=1, source_target_pairs={{0,15},{1,0},{2,1},{3,2},{4,3},{5,4},{6,5},{7,6},{8,7},{9,8},{10,9... | collective-permute-start | bytes 393224 | tf_op jit(solution)/shard_map/ppermute | solution.py:35
  18.0 0.9 copy-start
  18.9 5.4 %collective-permute-start.2 = (f32[4,64,128]{2,1,0:T(8,128)S(1)}, f32[4,64,128]{2,1,0:T(8,128)S(1)}, u32[]{:S(2)}, u32[]{:S(2)}) collective-permute-start(f32[4,64,128]{2,1,0:T(8,128)S(1)} %collective-permute-done), channel_id=1, source_target_pairs={{0,1},{1,2},{2,3},{3,4},{4,5},{5,6},{6,7},{7,8},{8,9},{9,10},{10,1... | collective-permute-start | bytes 393224 | tf_op jit(solution)/shard_map/ppermute | solution.py:28
  19.0 5.4 %collective-permute-start.3 = (f32[4,64,128]{2,1,0:T(8,128)S(1)}, f32[4,64,128]{2,1,0:T(8,128)S(1)}, u32[]{:S(2)}, u32[]{:S(2)}) collective-permute-start(f32[4,64,128]{2,1,0:T(8,128)S(1)} %collective-permute-done.1), channel_id=1, source_target_pairs={{0,15},{1,0},{2,1},{3,2},{4,3},{5,4},{6,5},{7,6},{8,7},{9,8},{10,9... | collective-permute-start | bytes 393224 | tf_op jit(solution)/shard_map/ppermute | solution.py:35
  24.4 5.4 %collective-permute-start.4 = (f32[4,64,128]{2,1,0:T(8,128)S(1)}, f32[4,64,128]{2,1,0:T(8,128)S(1)}, u32[]{:S(2)}, u32[]{:S(2)}) collective-permute-start(f32[4,64,128]{2,1,0:T(8,128)S(1)} %collective-permute-done.2), channel_id=1, source_target_pairs={{0,1},{1,2},{2,3},{3,4},{4,5},{5,6},{6,7},{7,8},{8,9},{9,10},{10,1... | collective-permute-start | bytes 393224 | tf_op jit(solution)/shard_map/ppermute | solution.py:28
  24.4 5.4 %collective-permute-start.5 = (f32[4,64,128]{2,1,0:T(8,128)S(1)}, f32[4,64,128]{2,1,0:T(8,128)S(1)}, u32[]{:S(2)}, u32[]{:S(2)}) collective-permute-start(f32[4,64,128]{2,1,0:T(8,128)S(1)} %collective-permute-done.3), channel_id=1, source_target_pairs={{0,15},{1,0},{2,1},{3,2},{4,3},{5,4},{6,5},{7,6},{8,7},{9,8},{10,9... | collective-permute-start | bytes 393224 | tf_op jit(solution)/shard_map/ppermute | solution.py:35
  29.8 5.4 %collective-permute-start.6 = (f32[4,64,128]{2,1,0:T(8,128)S(1)}, f32[4,64,128]{2,1,0:T(8,128)S(1)}, u32[]{:S(2)}, u32[]{:S(2)}) collective-permute-start(f32[4,64,128]{2,1,0:T(8,128)S(1)} %collective-permute-done.4), channel_id=1, source_target_pairs={{0,1},{1,2},{2,3},{3,4},{4,5},{5,6},{6,7},{7,8},{8,9},{9,10},{10,1... | collective-permute-start | bytes 393224 | tf_op jit(solution)/shard_map/ppermute | solution.py:28
  29.8 5.4 %collective-permute-start.7 = (f32[4,64,128]{2,1,0:T(8,128)S(1)}, f32[4,64,128]{2,1,0:T(8,128)S(1)}, u32[]{:S(2)}, u32[]{:S(2)}) collective-permute-start(f32[4,64,128]{2,1,0:T(8,128)S(1)} %collective-permute-done.5), channel_id=1, source_target_pairs={{0,15},{1,0},{2,1},{3,2},{4,3},{5,4},{6,5},{7,6},{8,7},{9,8},{10,9... | collective-permute-start | bytes 393224 | tf_op jit(solution)/shard_map/ppermute | solution.py:35
  35.2 5.4 %collective-permute-start.8 = (f32[4,64,128]{2,1,0:T(8,128)S(1)}, f32[4,64,128]{2,1,0:T(8,128)S(1)}, u32[]{:S(2)}, u32[]{:S(2)}) collective-permute-start(f32[4,64,128]{2,1,0:T(8,128)S(1)} %collective-permute-done.6), channel_id=1, source_target_pairs={{0,1},{1,2},{2,3},{3,4},{4,5},{5,6},{6,7},{7,8},{8,9},{9,10},{10,1... | collective-permute-start | bytes 393224 | tf_op jit(solution)/shard_map/ppermute | solution.py:28
  35.2 5.4 %collective-permute-start.9 = (f32[4,64,128]{2,1,0:T(8,128)S(1)}, f32[4,64,128]{2,1,0:T(8,128)S(1)}, u32[]{:S(2)}, u32[]{:S(2)}) collective-permute-start(f32[4,64,128]{2,1,0:T(8,128)S(1)} %collective-permute-done.7), channel_id=1, source_target_pairs={{0,15},{1,0},{2,1},{3,2},{4,3},{5,4},{6,5},{7,6},{8,7},{9,8},{10,9... | collective-permute-start | bytes 393224 | tf_op jit(solution)/shard_map/ppermute | solution.py:35
  40.6 5.4 %collective-permute-start.10 = (f32[4,64,128]{2,1,0:T(8,128)S(1)}, f32[4,64,128]{2,1,0:T(8,128)S(1)}, u32[]{:S(2)}, u32[]{:S(2)}) collective-permute-start(f32[4,64,128]{2,1,0:T(8,128)S(1)} %collective-permute-done.8), channel_id=1, source_target_pairs={{0,1},{1,2},{2,3},{3,4},{4,5},{5,6},{6,7},{7,8},{8,9},{9,10},{10,1... | collective-permute-start | bytes 393224 | tf_op jit(solution)/shard_map/ppermute | solution.py:28
  40.6 5.4 %collective-permute-start.11 = (f32[4,64,128]{2,1,0:T(8,128)S(1)}, f32[4,64,128]{2,1,0:T(8,128)S(1)}, u32[]{:S(2)}, u32[]{:S(2)}) collective-permute-start(f32[4,64,128]{2,1,0:T(8,128)S(1)} %collective-permute-done.9), channel_id=1, source_target_pairs={{0,15},{1,0},{2,1},{3,2},{4,3},{5,4},{6,5},{7,6},{8,7},{9,8},{10,9... | collective-permute-start | bytes 393224 | tf_op jit(solution)/shard_map/ppermute | solution.py:35
  46.0 5.4 %collective-permute-start.12 = (f32[4,64,128]{2,1,0:T(8,128)S(1)}, f32[4,64,128]{2,1,0:T(8,128)S(1)}, u32[]{:S(2)}, u32[]{:S(2)}) collective-permute-start(f32[4,64,128]{2,1,0:T(8,128)S(1)} %collective-permute-done.10), channel_id=1, source_target_pairs={{0,1},{1,2},{2,3},{3,4},{4,5},{5,6},{6,7},{7,8},{8,9},{9,10},{10,1... | collective-permute-start | bytes 393224 | tf_op jit(solution)/shard_map/ppermute | solution.py:28
  46.0 5.4 %collective-permute-start.13 = (f32[4,64,128]{2,1,0:T(8,128)S(1)}, f32[4,64,128]{2,1,0:T(8,128)S(1)}, u32[]{:S(2)}, u32[]{:S(2)}) collective-permute-start(f32[4,64,128]{2,1,0:T(8,128)S(1)} %collective-permute-done.11), channel_id=1, source_target_pairs={{0,15},{1,0},{2,1},{3,2},{4,3},{5,4},{6,5},{7,6},{8,7},{9,8},{10,9... | collective-permute-start | bytes 393224 | tf_op jit(solution)/shard_map/ppermute | solution.py:35
  51.3 5.3 %collective-permute-start.14 = (f32[4,64,128]{2,1,0:T(8,128)S(1)}, f32[4,64,128]{2,1,0:T(8,128)S(1)}, u32[]{:S(2)}, u32[]{:S(2)}) collective-permute-start(f32[4,64,128]{2,1,0:T(8,128)S(1)} %collective-permute-done.12), channel_id=1, source_target_pairs={{0,1},{1,2},{2,3},{3,4},{4,5},{5,6},{6,7},{7,8},{8,9},{9,10},{10,1... | collective-permute-start | bytes 393224 | tf_op jit(solution)/shard_map/ppermute | solution.py:28
  59.4 6.5 %copy-start.3 = (s32[128]{0:T(128)S(1)}, s32[128]{0:T(128)}, u32[]{:S(2)}) copy-start(s32[128]{0:T(128)} %param.10) | copy-start | bytes 1540
  66.0 4.5 %copy-start.2 = (f32[256]{0:T(256)S(1)}, f32[256]{0:T(256)}, u32[]{:S(2)}) copy-start(f32[256]{0:T(256)} %param.8) | copy-start | bytes 3076
  70.5 101.2 %copy-start.1 = (f32[256,128]{1,0:T(8,128)}, f32[256,128]{1,0:T(8,128)S(1)}, u32[]{:S(2)}) copy-start(f32[256,128]{1,0:T(8,128)S(1)} %multiply_add_fusion) | copy-start | bytes 393220
Sparse Core Ops, SparseCore 0:
  71.7 98.4 all-reduce.1
